TPU v7x, 32 devices: a whole 2x2x4 slice. The times are simulated.
32 devices in a mesh: dp: 8 (over z, x), tensor: 4 (over y, core).
Axes of the slice: x: 2, y: 2, z: 4, core: 2. Of those that a mesh axis runs over, the one named last changes fastest.
Arguments:
- gate_grads: bfloat16 [8, 256, 8192], P('dp', 'tensor'), may hold values from -6 to 6
- up_grads: bfloat16 [8, 256, 8192], P('dp', 'tensor'), may hold values from -6 to 6
- gate_errors: bfloat16 [8, 256, 8192], P('dp', 'tensor'), may hold values from -3 to 3
- up_errors: bfloat16 [8, 256, 8192], P('dp', 'tensor'), may hold values from -3 to 3
- gate_start: float32 [8192, 32], replicated, may hold values from -6 to 6
- up_start: float32 [8192, 32], replicated, may hold values from -6 to 6
Outputs:
- gate_mean: bfloat16 [256, 8192], P('tensor')
- up_mean: bfloat16 [256, 8192], P('tensor')
- gate_new_errors: bfloat16 [8, 256, 8192], P('dp', 'tensor')
- up_new_errors: bfloat16 [8, 256, 8192], P('dp', 'tensor')
All inputs are finite; a program needn't handle non-finite values.
Results may differ from a plain program's by a relative error of at most 0.0015.
Values sent between devices are 32-bit elements; how exact they have to be, the bound alone decides.
A program may use at most 64 MiB of HBM per device.

v0:
```python
import jax
import jax.numpy as jnp
from jax import lax
from jax.sharding import PartitionSpec as P


def orthonormal(left, gram):
    lower = jnp.linalg.cholesky(gram)
    return lax.linalg.triangular_solve(lower, left, left_side=False, lower=True, transpose_a=True)


def inner(first, second):
    return jnp.dot(first.T, second, precision=lax.Precision.HIGHEST)


def per_device(gate_grads, up_grads, gate_errors, up_errors, gate_start, up_start):
    replicas = lax.axis_size("dp")
    gate_full = gate_grads[0].astype(jnp.float32) + gate_errors[0].astype(jnp.float32)
    up_full = up_grads[0].astype(jnp.float32) + up_errors[0].astype(jnp.float32)
    gate_term = jnp.dot(gate_full, gate_start, precision=lax.Precision.HIGHEST)
    up_term = jnp.dot(up_full, up_start, precision=lax.Precision.HIGHEST)
    gate_left, up_left = lax.psum((gate_term, up_term), "dp")
    gate_left = gate_left / replicas
    up_left = up_left / replicas
    gate_gram, up_gram = lax.psum((inner(gate_left, gate_left), inner(up_left, up_left)), "tensor")
    gate_basis = orthonormal(gate_left, gate_gram)
    up_basis = orthonormal(up_left, up_gram)
    gate_right, up_right = lax.psum(
        (inner(gate_full, gate_basis), inner(up_full, up_basis)), ("dp", "tensor")
    )
    gate_right = gate_right / replicas
    up_right = up_right / replicas
    gate_approx = jnp.dot(gate_basis, gate_right.T, precision=lax.Precision.HIGHEST)
    up_approx = jnp.dot(up_basis, up_right.T, precision=lax.Precision.HIGHEST)
    gate_new = (gate_full - gate_approx).astype(jnp.bfloat16)[None]
    up_new = (up_full - up_approx).astype(jnp.bfloat16)[None]
    return (gate_approx.astype(jnp.bfloat16), up_approx.astype(jnp.bfloat16), gate_new, up_new)


def solution(mesh):
    in_specs = (
        P("dp", "tensor", None),
        P("dp", "tensor", None),
        P("dp", "tensor", None),
        P("dp", "tensor", None),
        P(),
        P(),
    )
    out_specs = (
        P("tensor", None),
        P("tensor", None),
        P("dp", "tensor", None),
        P("dp", "tensor", None),
    )
    return jax.shard_map(
        per_device, mesh=mesh, in_specs=in_specs, out_specs=out_specs, check_vma=False
    )
```

profile of v0, /device:TPU:0, one launch (start us, length us, event | category | flops | bytes accessed | tf_op | source)
XLA Modules:
  0.0 229.0 jit_solution(3288730595172913577)
XLA Ops:
  7.2 0.0 copy-start
  7.2 0.0 all-reduce.5.cloned.1.call-start
  7.2 1.2 copy-done
  8.4 0.0 copy-start.3
  8.4 0.0 copy-start.6
  8.4 0.0 copy-start.9
  8.4 3.6 %fusion.7 = f32[64,32]{0,1:T(8,128)S(1)} fusion(f32[8192,32]{0,1:T(8,128)S(1)} %copy-done, bf16[1,64,8192]{2,1,0:T(8,128)(2,1)} %param.11, bf16[1,64,8192]{2,1,0:T(8,128)(2,1)} %param.9), kind=kOutput, calls=%fused_computation.9 | convolution fusion | flops 202899456 | bytes 3153920 | tf_op jit(solution)/shard_map/dot_general | solution.py:20
  12.0 0.0 copy-done.3
  12.0 0.0 copy-done.6
  12.0 0.0 copy-done.9
  12.0 0.0 copy-start.1
  12.0 0.0 copy-start.2
  12.0 1.9 fusion.2
  14.0 38.8 %all-reduce.1 = (f32[64,32]{0,1:T(8,128)S(1)}, f32[64,32]{0,1:T(8,128)S(1)}) all-reduce(f32[64,32]{0,1:T(8,128)S(1)} %fusion.7, f32[64,32]{0,1:T(8,128)S(1)} %fusion.2), channel_id=1, replica_groups=mesh['dp'=8,'tensor'=4] {'dp'}, use_global_device_ids=true, to_apply=%region_0.0 | all-reduce | flops 4096 | bytes 32768 | tf_op jit(solution)/shard_map/psum | solution.py:22
  52.8 0.1 fusion.28
  52.9 0.1 fusion.25
  53.1 10.5 %all-reduce.2 = (f32[32,32]{0,1:T(8,128)S(1)}, f32[32,32]{0,1:T(8,128)S(1)}) all-reduce(f32[32,32]{0,1:T(8,128)S(1)} %fusion.28, f32[32,32]{0,1:T(8,128)S(1)} %fusion.25), channel_id=1, replica_groups=mesh['dp'=8,'tensor'=4] {'tensor'}, use_global_device_ids=true, to_apply=%region_1.0 | all-reduce | flops 2048 | bytes 16384 | tf_op jit(solution)/shard_map/psum | solution.py:25
  63.6 0.1 copy.15
  63.6 0.1 copy.17
  63.7 2.9 %cholesky.55 = f32[32,32]{1,0:T(8,128)S(1)} custom-call(f32[32,32]{1,0:T(8,128)S(1)} %get-tuple-element.16), custom_call_target="Cholesky" | custom-call | tf_op jit(solution)/shard_map/jit(cholesky)/cholesky | solution.py:8
  66.7 0.6 compare_reduce_fusion
  67.3 0.7 fusion.19
  68.0 2.4 %custom-call.7 = f32[1,32,32]{1,2,0:T(8,128)S(1)} custom-call(f32[1,32,32]{2,1,0:T(8,128)S(1)} %fusion.19), custom_call_target="InvertDiagBlocksLowerTriangular" | custom-call | tf_op jit(solution)/shard_map/triangular_solve/custom-call.0 | solution.py:9
  70.4 0.2 convolution_bitcast_fusion
  70.7 2.9 %cholesky.44 = f32[32,32]{1,0:T(8,128)S(1)} custom-call(f32[32,32]{1,0:T(8,128)S(1)} %get-tuple-element.17), custom_call_target="Cholesky" | custom-call | tf_op jit(solution)/shard_map/jit(cholesky)/cholesky | solution.py:8
  73.6 0.6 compare_reduce_fusion.1
  74.3 0.7 fusion.18
  74.9 2.4 %custom-call.6 = f32[1,32,32]{1,2,0:T(8,128)S(1)} custom-call(f32[1,32,32]{2,1,0:T(8,128)S(1)} %fusion.18), custom_call_target="InvertDiagBlocksLowerTriangular" | custom-call | tf_op jit(solution)/shard_map/triangular_solve/custom-call.0 | solution.py:9
  77.4 0.2 convolution_bitcast_fusion.1
  77.6 0.0 copy-done.1
  77.6 0.0 copy-done.2
  77.6 0.0 copy-start.4
  77.6 0.0 copy-start.7
  77.6 2.5 %fusion.5 = f32[8192,32]{0,1:T(8,128)} fusion(f32[64,32]{0,1:T(8,128)S(1)} %convolution_bitcast_fusion.1, bf16[1,64,8192]{2,1,0:T(8,128)(2,1)S(1)} %copy-done.1, bf16[1,64,8192]{2,1,0:T(8,128)(2,1)S(1)} %copy-done.2), kind=kOutput, calls=%fused_computation.7 | convolution fusion | flops 202899456 | bytes 3153920 | tf_op jit(solution)/shard_map/dot_general | solution.py:13
  80.1 0.0 copy-done.4
  80.1 0.0 copy-done.7
  80.1 2.5 %fusion = f32[8192,32]{0,1:T(8,128)} fusion(f32[64,32]{0,1:T(8,128)S(1)} %convolution_bitcast_fusion, bf16[1,64,8192]{2,1,0:T(8,128)(2,1)S(1)} %copy-done.4, bf16[1,64,8192]{2,1,0:T(8,128)(2,1)S(1)} %copy-done.7), kind=kOutput, calls=%fused_computation.1 | convolution fusion | flops 202899456 | bytes 3153920 | tf_op jit(solution)/shard_map/dot_general | solution.py:13
  82.6 0.0 all-reduce.5.cloned.1.call-update
  82.6 131.5 %all-reduce.5.cloned.1.call-done = (f32[8192,32]{0,1:T(8,128)}, f32[8192,32]{0,1:T(8,128)}) async-done(((f32[8192,32]{0,1:T(8,128)}, f32[8192,32]{0,1:T(8,128)}), (f32[8192,32]{0,1:T(8,128)}, f32[8192,32]{0,1:T(8,128)})) %all-reduce.5.cloned.1.call-update) | async-done | bytes 2097168 | tf_op jit(solution)/shard_map/psum | solution.py:28
  214.1 0.0 copy-start.5
  214.1 0.0 copy-start.8
  214.1 0.0 copy-start.10
  214.1 4.7 %fusion.10 = (bf16[1,64,8192]{2,1,0:T(8,128)(2,1)}, bf16[64,8192]{1,0:T(8,128)(2,1)}) fusion(bf16[1,64,8192]{2,1,0:T(8,128)(2,1)S(1)} %copy-done.1, bf16[1,64,8192]{2,1,0:T(8,128)(2,1)S(1)} %copy-done.2, f32[64,32]{0,1:T(8,128)S(1)} %convolution_bitcast_fusion.1, f32[8192,32]{0,1:T(8,128)} %get-tuple-element.6), kind=kOutput, calls=%fused_computation.16 | convolution fusion | flops 204734464 | bytes 5251072 | tf_op jit(solution)/shard_map/dot_general | solution.py:33
  218.8 0.0 copy-done.5
  218.8 0.0 copy-done.8
  218.8 0.0 copy-done.10
  218.8 3.4 %fusion.11 = (bf16[1,64,8192]{2,1,0:T(8,128)(2,1)}, bf16[64,8192]{1,0:T(8,128)(2,1)}) fusion(bf16[1,64,8192]{2,1,0:T(8,128)(2,1)S(1)} %copy-done.5, bf16[1,64,8192]{2,1,0:T(8,128)(2,1)S(1)} %copy-done.8, f32[64,32]{0,1:T(8,128)S(1)} %convolution_bitcast_fusion, f32[8192,32]{0,1:T(8,128)S(1)} %copy-done.10), kind=kOutput, calls=%fused_computation.17 | convolution fusion | flops 204734464 | bytes 5251072 | tf_op jit(solution)/shard_map/dot_general | solution.py:34
  (3 shorter events, 0.1 us)
Async XLA Ops:
  7.2 1.2 copy-start
  7.2 206.9 %all-reduce.5.cloned.1.call-start = ((), (), s32[]{:S(2)}) async-start(), calls=%async_computation | async-start | bytes 4194304 | tf_op jit(solution)/shard_map/psum | solution.py:28
  8.4 3.6 %copy-start.3 = (bf16[1,64,8192]{2,1,0:T(8,128)(2,1)S(1)}, bf16[1,64,8192]{2,1,0:T(8,128)(2,1)}, u32[]{:S(2)}) copy-start(bf16[1,64,8192]{2,1,0:T(8,128)(2,1)} %param.12) | copy-start | bytes 3145732
  8.4 3.6 %copy-start.6 = (bf16[1,64,8192]{2,1,0:T(8,128)(2,1)S(1)}, bf16[1,64,8192]{2,1,0:T(8,128)(2,1)}, u32[]{:S(2)}) copy-start(bf16[1,64,8192]{2,1,0:T(8,128)(2,1)} %param.10) | copy-start | bytes 3145732
  8.4 3.6 %copy-start.9 = (f32[8192,32]{0,1:T(8,128)S(1)}, f32[8192,32]{0,1:T(8,128)}, u32[]{:S(2)}) copy-start(f32[8192,32]{0,1:T(8,128)} %param.14) | copy-start | bytes 3145732
  12.0 65.6 %copy-start.1 = (bf16[1,64,8192]{2,1,0:T(8,128)(2,1)S(1)}, bf16[1,64,8192]{2,1,0:T(8,128)(2,1)}, u32[]{:S(2)}) copy-start(bf16[1,64,8192]{2,1,0:T(8,128)(2,1)} %param.11) | copy-start | bytes 3145732
  12.0 65.6 %copy-start.2 = (bf16[1,64,8192]{2,1,0:T(8,128)(2,1)S(1)}, bf16[1,64,8192]{2,1,0:T(8,128)(2,1)}, u32[]{:S(2)}) copy-start(bf16[1,64,8192]{2,1,0:T(8,128)(2,1)} %param.9) | copy-start | bytes 3145732
  77.6 2.5 %copy-start.4 = (bf16[1,64,8192]{2,1,0:T(8,128)(2,1)S(1)}, bf16[1,64,8192]{2,1,0:T(8,128)(2,1)}, u32[]{:S(2)}) copy-start(bf16[1,64,8192]{2,1,0:T(8,128)(2,1)} %param.12) | copy-start | bytes 3145732
  77.6 2.5 %copy-start.7 = (bf16[1,64,8192]{2,1,0:T(8,128)(2,1)S(1)}, bf16[1,64,8192]{2,1,0:T(8,128)(2,1)}, u32[]{:S(2)}) copy-start(bf16[1,64,8192]{2,1,0:T(8,128)(2,1)} %param.10) | copy-start | bytes 3145732
  214.1 4.7 %copy-start.5 = (bf16[1,64,8192]{2,1,0:T(8,128)(2,1)S(1)}, bf16[1,64,8192]{2,1,0:T(8,128)(2,1)}, u32[]{:S(2)}) copy-start(bf16[1,64,8192]{2,1,0:T(8,128)(2,1)} %param.12) | copy-start | bytes 3145732
  214.1 4.7 %copy-start.8 = (bf16[1,64,8192]{2,1,0:T(8,128)(2,1)S(1)}, bf16[1,64,8192]{2,1,0:T(8,128)(2,1)}, u32[]{:S(2)}) copy-start(bf16[1,64,8192]{2,1,0:T(8,128)(2,1)} %param.10) | copy-start | bytes 3145732
  214.1 4.7 %copy-start.10 = (f32[8192,32]{0,1:T(8,128)S(1)}, f32[8192,32]{0,1:T(8,128)}, u32[]{:S(2)}) copy-start(f32[8192,32]{0,1:T(8,128)} %get-tuple-element.7) | copy-start | bytes 3145732
Sparse Core Ops, SparseCore 0:
  82.8 131.3 all-reduce.4
where the time goes:
time: 229 us
  waiting for transfers between devices  132 us (58%)
  blocking collectives  49.3 us (22%)
  matrix products  19.3 us (8%)
  between operations  14.2 us (6%)
  other arithmetic  13.4 us (6%)
    psum x1, waiting for transfers between devices, per_device(): lax.psum((inner(gate_full, gate_basis), inner(up_full, up_basis)), ('dp',...  131 us
    psum x1, blocking collectives, per_device(): gate_left, up_left = lax.psum((gate_term, up_term), 'dp')  38.8 us
    psum x1, blocking collectives, per_device(): lax.psum((inner(gate_left, gate_left), inner(up_left, up_left)), 'tensor')  10.5 us
    another operation x6, other arithmetic, orthonormal(): lower = jnp.linalg.cholesky(gram)  7.18 us
    another operation x4, other arithmetic, orthonormal(): lax.linalg.triangular_solve(lower, left, left_side=False, lower=True, tra...  6.17 us
    dot_general x4, matrix products, inner(): return jnp.dot(first.T, second, precision=lax.Precision.HIGHEST)  5.27 us
    dot_general x1, matrix products, per_device(): jnp.dot(gate_basis, gate_right.T, precision=lax.Precision.HIGHEST)  4.68 us
  transfers between devices with their start and end apart: 1, of which 1 were waited for; matrix products, arithmetic and copies ran while one was open for 0% of the time, Pallas kernels for 0%

commit v1 on v0

--- a/solution.py
+++ b/solution.py
@@ -26,7 +26,7 @@
     gate_basis = orthonormal(gate_left, gate_gram)
     up_basis = orthonormal(up_left, up_gram)
     gate_right, up_right = lax.psum(
-        (inner(gate_full, gate_basis), inner(up_full, up_basis)), ("dp", "tensor")
+        lax.psum((inner(gate_full, gate_basis), inner(up_full, up_basis)), "tensor"), "dp"
     )
     gate_right = gate_right / replicas
     up_right = up_right / replicas

time: 229 us -> 253 us (1.10)
  waiting for transfers between devices: 132 us -> 155 us
    psum x1 -> x2, waiting for transfers between devices: 131 us -> 155 us  [the longest x1 106 us: per_device(): lax.psum(lax.psum((inner(gate_full, gate_basis), inner(up_full, up_basis)...]
  transfers between devices with their start and end apart: 1 -> 2, of which waited for: 1 -> 2; matrix products, arithmetic and copies ran while one was open for 0% -> 0% of each run, Pallas kernels for 0% -> 0%
where the time goes in v1:
time: 253 us
  waiting for transfers between devices  155 us (61%)
  blocking collectives  49.1 us (19%)
  matrix products  19.3 us (8%)
  between operations  14.2 us (6%)
  other arithmetic  13.4 us (5%)
    psum x1, waiting for transfers between devices, per_device(): lax.psum(lax.psum((inner(gate_full, gate_basis), inner(up_full, up_basis)...  106 us
    psum x1, waiting for transfers between devices, per_device(): lax.psum((inner(gate_full, gate_basis), inner(up_full, up_basis)), 'tensor')  48.9 us
    psum x1, blocking collectives, per_device(): gate_left, up_left = lax.psum((gate_term, up_term), 'dp')  38.8 us
    psum x1, blocking collectives, per_device(): lax.psum((inner(gate_left, gate_left), inner(up_left, up_left)), 'tensor')  10.3 us
    another operation x6, other arithmetic, orthonormal(): lower = jnp.linalg.cholesky(gram)  7.18 us
    another operation x4, other arithmetic, orthonormal(): lax.linalg.triangular_solve(lower, left, left_side=False, lower=True, tra...  6.17 us
    dot_general x4, matrix products, inner(): return jnp.dot(first.T, second, precision=lax.Precision.HIGHEST)  5.26 us
  transfers between devices with their start and end apart: 2, of which 2 were waited for; matrix products, arithmetic and copies ran while one was open for 0% of the time, Pallas kernels for 0%

profile of v1, /device:TPU:0, one launch (start us, length us, event | category | flops | bytes accessed | tf_op | source)
XLA Modules:
  0.0 252.9 jit_solution(13856586069592327271)
XLA Ops:
  7.2 0.0 copy-start
  7.2 0.0 all-reduce.9.cloned.1.call-start
  7.2 1.2 copy-done
  8.4 0.0 copy-start.3
  8.4 0.0 copy-start.6
  8.4 0.0 copy-start.9
  8.4 3.6 %fusion.7 = f32[64,32]{0,1:T(8,128)S(1)} fusion(f32[8192,32]{0,1:T(8,128)S(1)} %copy-done, bf16[1,64,8192]{2,1,0:T(8,128)(2,1)} %param.11, bf16[1,64,8192]{2,1,0:T(8,128)(2,1)} %param.9), kind=kOutput, calls=%fused_computation.9 | convolution fusion | flops 202899456 | bytes 3153920 | tf_op jit(solution)/shard_map/dot_general | solution.py:20
  12.0 0.0 copy-done.3
  12.0 0.0 copy-done.6
  12.0 0.0 copy-done.9
  12.0 0.0 copy-start.1
  12.0 0.0 copy-start.2
  12.0 1.9 fusion.2
  14.0 38.8 %all-reduce = (f32[64,32]{0,1:T(8,128)S(1)}, f32[64,32]{0,1:T(8,128)S(1)}) all-reduce(f32[64,32]{0,1:T(8,128)S(1)} %fusion.7, f32[64,32]{0,1:T(8,128)S(1)} %fusion.2), channel_id=1, replica_groups=mesh['dp'=8,'tensor'=4] {'dp'}, use_global_device_ids=true, to_apply=%region_0.0 | all-reduce | flops 4096 | bytes 32768 | tf_op jit(solution)/shard_map/psum | solution.py:22
  52.8 0.1 fusion.28
  52.9 0.1 fusion.25
  53.1 10.3 %all-reduce.2 = (f32[32,32]{0,1:T(8,128)S(1)}, f32[32,32]{0,1:T(8,128)S(1)}) all-reduce(f32[32,32]{0,1:T(8,128)S(1)} %fusion.28, f32[32,32]{0,1:T(8,128)S(1)} %fusion.25), channel_id=1, replica_groups=mesh['dp'=8,'tensor'=4] {'tensor'}, use_global_device_ids=true, to_apply=%region_1.0 | all-reduce | flops 2048 | bytes 16384 | tf_op jit(solution)/shard_map/psum | solution.py:25
  63.4 0.1 copy.15
  63.5 0.1 copy.17
  63.6 2.9 %cholesky.55 = f32[32,32]{1,0:T(8,128)S(1)} custom-call(f32[32,32]{1,0:T(8,128)S(1)} %get-tuple-element.18), custom_call_target="Cholesky" | custom-call | tf_op jit(solution)/shard_map/jit(cholesky)/cholesky | solution.py:8
  66.5 0.6 compare_reduce_fusion
  67.2 0.7 fusion.19
  67.8 2.4 custom-call.7
  70.2 0.2 convolution_bitcast_fusion
  70.5 2.9 %cholesky.44 = f32[32,32]{1,0:T(8,128)S(1)} custom-call(f32[32,32]{1,0:T(8,128)S(1)} %get-tuple-element.19), custom_call_target="Cholesky" | custom-call | tf_op jit(solution)/shard_map/jit(cholesky)/cholesky | solution.py:8
  73.4 0.6 compare_reduce_fusion.1
  74.1 0.7 fusion.18
  74.7 2.4 custom-call.6
  77.2 0.2 convolution_bitcast_fusion.1
  77.4 0.0 copy-done.1
  77.4 0.0 copy-done.2
  77.4 0.0 copy-start.4
  77.4 0.0 copy-start.7
  77.5 2.5 fusion.5
  80.0 0.0 copy-done.4
  80.0 0.0 copy-done.7
  80.0 2.5 fusion
  82.4 0.0 all-reduce.9.cloned.1.call-update
  82.5 0.2 all-reduce.7.cloned.1.call-start
  82.7 48.9 %all-reduce.9.cloned.1.call-done = (f32[8192,32]{0,1:T(8,128)}, f32[8192,32]{0,1:T(8,128)}) async-done(((f32[8192,32]{0,1:T(8,128)}, f32[8192,32]{0,1:T(8,128)}), (f32[8192,32]{0,1:T(8,128)}, f32[8192,32]{0,1:T(8,128)})) %all-reduce.9.cloned.1.call-update) | async-done | bytes 2097168 | tf_op jit(solution)/shard_map/psum | solution.py:29
  131.6 0.0 all-reduce.7.cloned.1.call-update
  131.6 106.4 %all-reduce.7.cloned.1.call-done = (f32[8192,32]{0,1:T(8,128)}, f32[8192,32]{0,1:T(8,128)}) async-done(((f32[8192,32]{0,1:T(8,128)}, f32[8192,32]{0,1:T(8,128)}), (f32[8192,32]{0,1:T(8,128)}, f32[8192,32]{0,1:T(8,128)})) %all-reduce.7.cloned.1.call-update) | async-done | bytes 2097168 | tf_op jit(solution)/shard_map/psum | solution.py:28
  238.0 0.0 copy-start.5
  238.0 4.7 %fusion.10 = (bf16[1,64,8192]{2,1,0:T(8,128)(2,1)}, bf16[64,8192]{1,0:T(8,128)(2,1)}) fusion(bf16[1,64,8192]{2,1,0:T(8,128)(2,1)S(1)} %copy-done.1, bf16[1,64,8192]{2,1,0:T(8,128)(2,1)S(1)} %copy-done.2, f32[64,32]{0,1:T(8,128)S(1)} %convolution_bitcast_fusion.1, f32[8192,32]{0,1:T(8,128)} %get-tuple-element.8), kind=kOutput, calls=%fused_computation.16 | convolution fusion | flops 204734464 | bytes 5251072 | tf_op jit(solution)/shard_map/dot_general | solution.py:33
  242.7 0.0 copy-done.5
  242.7 0.0 copy-done.8
  242.7 0.0 copy-done.10
  242.7 3.4 %fusion.11 = (bf16[1,64,8192]{2,1,0:T(8,128)(2,1)}, bf16[64,8192]{1,0:T(8,128)(2,1)}) fusion(bf16[1,64,8192]{2,1,0:T(8,128)(2,1)S(1)} %copy-done.5, bf16[1,64,8192]{2,1,0:T(8,128)(2,1)S(1)} %copy-done.8, f32[64,32]{0,1:T(8,128)S(1)} %convolution_bitcast_fusion, f32[8192,32]{0,1:T(8,128)S(1)} %copy-done.10), kind=kOutput, calls=%fused_computation.17 | convolution fusion | flops 204734464 | bytes 5251072 | tf_op jit(solution)/shard_map/dot_general | solution.py:34
  (5 shorter events, 0.1 us)
Async XLA Ops:
  7.2 1.2 copy-start
  7.2 124.4 %all-reduce.9.cloned.1.call-start = ((), (), s32[]{:S(2)}) async-start(), calls=%async_computation.1 | async-start | bytes 4194304 | tf_op jit(solution)/shard_map/psum | solution.py:29
  8.4 3.6 %copy-start.3 = (bf16[1,64,8192]{2,1,0:T(8,128)(2,1)S(1)}, bf16[1,64,8192]{2,1,0:T(8,128)(2,1)}, u32[]{:S(2)}) copy-start(bf16[1,64,8192]{2,1,0:T(8,128)(2,1)} %param.12) | copy-start | bytes 3145732
  8.4 3.6 %copy-start.6 = (bf16[1,64,8192]{2,1,0:T(8,128)(2,1)S(1)}, bf16[1,64,8192]{2,1,0:T(8,128)(2,1)}, u32[]{:S(2)}) copy-start(bf16[1,64,8192]{2,1,0:T(8,128)(2,1)} %param.10) | copy-start | bytes 3145732
  8.4 3.6 %copy-start.9 = (f32[8192,32]{0,1:T(8,128)S(1)}, f32[8192,32]{0,1:T(8,128)}, u32[]{:S(2)}) copy-start(f32[8192,32]{0,1:T(8,128)} %param.14) | copy-start | bytes 3145732
  12.0 65.4 %copy-start.1 = (bf16[1,64,8192]{2,1,0:T(8,128)(2,1)S(1)}, bf16[1,64,8192]{2,1,0:T(8,128)(2,1)}, u32[]{:S(2)}) copy-start(bf16[1,64,8192]{2,1,0:T(8,128)(2,1)} %param.11) | copy-start | bytes 3145732
  12.0 65.4 %copy-start.2 = (bf16[1,64,8192]{2,1,0:T(8,128)(2,1)S(1)}, bf16[1,64,8192]{2,1,0:T(8,128)(2,1)}, u32[]{:S(2)}) copy-start(bf16[1,64,8192]{2,1,0:T(8,128)(2,1)} %param.9) | copy-start | bytes 3145732
  77.4 2.5 copy-start.4
  77.4 2.5 copy-start.7
  82.5 155.5 %all-reduce.7.cloned.1.call-start = ((), (), s32[]{:S(2)}) async-start(), calls=%async_computation | async-start | bytes 4194304 | tf_op jit(solution)/shard_map/psum | solution.py:28
  238.0 4.7 %copy-start.5 = (bf16[1,64,8192]{2,1,0:T(8,128)(2,1)S(1)}, bf16[1,64,8192]{2,1,0:T(8,128)(2,1)}, u32[]{:S(2)}) copy-start(bf16[1,64,8192]{2,1,0:T(8,128)(2,1)} %param.12) | copy-start | bytes 3145732
  238.0 4.7 %copy-start.8 = (bf16[1,64,8192]{2,1,0:T(8,128)(2,1)S(1)}, bf16[1,64,8192]{2,1,0:T(8,128)(2,1)}, u32[]{:S(2)}) copy-start(bf16[1,64,8192]{2,1,0:T(8,128)(2,1)} %param.10) | copy-start | bytes 3145732
  238.0 4.7 %copy-start.10 = (f32[8192,32]{0,1:T(8,128)S(1)}, f32[8192,32]{0,1:T(8,128)}, u32[]{:S(2)}) copy-start(f32[8192,32]{0,1:T(8,128)} %get-tuple-element.9) | copy-start | bytes 3145732
Sparse Core Ops, SparseCore 0:
  82.6 48.9 all-reduce.8
  135.7 102.2 all-reduce.6
